TPU v7x, 256 devices: a whole 4x4x8 slice. The times are simulated.
256 devices in a mesh: path: 16 (over z, core), col: 16 (over y, x).
Axes of the slice: x: 4, y: 4, z: 8, core: 2. Of those that a mesh axis runs over, the one named last changes fastest.
Arguments:
- exposure: bfloat16 [65536, 16384], P('path', 'col'), may hold values from -127 to 127
- scales: float32 [128, 65536], P('col', 'path'), may hold values from 0.003 to 0.27, as said below
- sketch: bfloat16 [32, 16384], P(None, 'col'), may hold values from -0.046875 to 0.046875
Outputs:
- basis: float32 [32, 65536], P(None, 'path')
- projected: float32 [32, 16384], P(None, 'col')
Inputs may be any that keep to these rules, and one draw needn't show every extreme that they name: `scales`: positive.
All inputs are finite; a program needn't handle non-finite values.
Results may differ from a plain program's by a relative error of at most 0.0003.
Values sent between devices are 32-bit elements; how exact they have to be, the bound alone decides.
No kernel may reach another device: no remote copies, remote signals or barrier semaphores. Data moves between devices by JAX's collectives and lax.ppermute only.
A program may use at most 64 MiB of HBM per device.

v0:
```python
import jax
import jax.numpy as jnp
from jax import lax
from jax.sharding import PartitionSpec as P

HIGH = lax.Precision.HIGHEST


def per_device(exposure, scales, sketch):
    row_count = exposure.shape[0]
    block_count = scales.shape[0]
    codes = exposure.reshape(row_count, block_count, 128)
    sketch3 = sketch.reshape(sketch.shape[0], block_count, 128)
    parts = lax.dot_general(
        sketch3, codes, (((2,), (2,)), ((1,), (1,))), preferred_element_type=jnp.float32
    )
    partial_value = jnp.sum(parts * scales[:, None, :], axis=0)
    sketched = lax.psum(partial_value, "col")
    gram_total = lax.psum(jnp.dot(sketched, sketched.T, precision=HIGH), "path")
    factor = jnp.linalg.cholesky(gram_total)
    orthonormal = lax.linalg.triangular_solve(factor, sketched, left_side=True, lower=True)
    weighted = orthonormal[None, :, :] * scales[:, None, :]
    term = lax.dot_general(
        weighted, codes.astype(jnp.float32), (((2,), (0,)), ((0,), (1,))), precision=HIGH
    )
    local_proj = term.transpose(1, 0, 2).reshape(orthonormal.shape[0], block_count * 128)
    projected = lax.psum(local_proj, "path")
    total_paths = row_count * lax.axis_size("path")
    basis = orthonormal * jnp.sqrt(jnp.float32(total_paths))
    return (basis, projected)


def solution(mesh):
    placed = (P("path", "col"), P("col", "path"), P(None, "col"))
    return jax.shard_map(
        per_device,
        mesh=mesh,
        in_specs=placed,
        out_specs=(P(None, "path"), P(None, "col")),
        check_vma=False,
    )
```

profile of v0, /device:TPU:1, one launch (start us, length us, event | category | flops | bytes accessed | tf_op | source)
XLA Modules:
  0.0 293.7 jit_solution(8979144331565636396)
XLA Ops:
  7.2 0.0 copy-start
  7.2 0.0 copy-start.1
  7.2 0.0 all-reduce.3.cloned.1.call-start
  7.2 0.8 copy-done
  8.0 7.3 %fusion.12 = f32[32,4096]{1,0:T(8,128)} fusion(f32[8,4096]{1,0:T(8,128)} %param.4, bf16[4096,1024]{1,0:T(8,128)(2,1)} %param.3, bf16[32,1024]{1,0:T(8,128)(2,1)S(1)} %copy-done), kind=kOutput, calls=%fused_computation.10 | convolution fusion | flops 270401536 | bytes 9109504 | tf_op jit(solution)/shard_map/dot_general | solution.py:14
  15.3 0.0 all-reduce.3.cloned.1.call-update
  15.3 0.0 all-reduce.5.cloned.1.call-start
  15.3 97.9 %all-reduce.3.cloned.1.call-done = f32[32,4096]{1,0:T(8,128)} async-done(((f32[32,4096]{1,0:T(8,128)}), f32[32,4096]{1,0:T(8,128)}) %all-reduce.3.cloned.1.call-update) | async-done | bytes 524304 | tf_op jit(solution)/shard_map/psum | solution.py:18
  113.2 1.8 fusion.26
  115.0 45.4 %psum.22 = f32[32,32]{0,1:T(8,128)S(1)} all-reduce(f32[32,32]{0,1:T(8,128)S(1)} %fusion.26), channel_id=1, replica_groups=mesh['path'=16,'col'=16] {'path'}, use_global_device_ids=true, to_apply=%region_2.0 | all-reduce | flops 1024 | bytes 8192 | tf_op jit(solution)/shard_map/psum | solution.py:19
  160.4 0.1 copy.13
  160.5 2.9 cholesky.16
  163.5 0.6 compare_reduce_fusion
  164.1 0.7 fusion.22
  164.8 2.4 custom-call.6
  167.2 2.5 broadcast_multiply_fusion
  169.7 0.0 copy-done.1
  169.7 6.3 %fusion.15 = f32[8,4,8,128]{3,2,1,0:T(8,128)S(1)} fusion(f32[32,4096]{1,0:T(8,128)S(1)} %get-tuple-element.3, f32[8,4096]{1,0:T(8,128)S(1)} %copy-done.1, bf16[4096,1024]{1,0:T(8,128)(2,1)} %param.3), kind=kOutput, calls=%fused_computation.11 | convolution fusion | flops 1611661312 | bytes 9175040 | tf_op jit(solution)/shard_map/dot_general | solution.py:23
  176.0 0.7 copy.39
  176.7 0.0 all-reduce.5.cloned.1.call-update
  176.7 108.7 %all-reduce.5.cloned.1.call-done = f32[32,1024]{1,0:T(8,128)} async-done(((f32[32,1024]{1,0:T(8,128)}), f32[32,1024]{1,0:T(8,128)}) %all-reduce.5.cloned.1.call-update) | async-done | bytes 131088 | tf_op jit(solution)/shard_map/psum | solution.py:27
  285.3 1.6 copy.42
  (2 shorter events, 0.0 us)
Async XLA Ops:
  7.2 0.8 copy-start
  7.2 162.5 %copy-start.1 = (f32[8,4096]{1,0:T(8,128)S(1)}, f32[8,4096]{1,0:T(8,128)}, u32[]{:S(2)}) copy-start(f32[8,4096]{1,0:T(8,128)} %param.4) | copy-start | bytes 393220
  7.2 106.0 %all-reduce.3.cloned.1.call-start = ((), (), s32[]{:S(2)}) async-start(), calls=%async_computation | async-start | bytes 1048576 | tf_op jit(solution)/shard_map/psum | solution.py:18
  15.3 270.1 %all-reduce.5.cloned.1.call-start = ((), (), s32[]{:S(2)}) async-start(), calls=%async_computation.1 | async-start | bytes 262144 | tf_op jit(solution)/shard_map/psum | solution.py:27
Sparse Core Ops, SparseCore 0:
  15.4 97.7 all-reduce.2
  176.8 108.4 all-reduce.4
where the time goes:
time: 294 us
  waiting for transfers between devices  207 us (70%)
  blocking collectives  45.4 us (15%)
  matrix products  17.8 us (6%)
  between operations  14.1 us (5%)
  other arithmetic  6.69 us (2%)
  local copies, waits for them, and re-layouts  3.09 us (1%)
    psum x1, waiting for transfers between devices, per_device(): projected = lax.psum(local_proj, 'path')  109 us
    psum x1, waiting for transfers between devices, per_device(): sketched = lax.psum(partial_value, 'col')  97.9 us
    psum x1, blocking collectives, per_device(): gram_total = lax.psum(jnp.dot(sketched, sketched.T, precision=HIGH), 'path')  45.4 us
    dot_general x1, matrix products, per_device(): lax.dot_general(sketch3, codes, (((2,), (2,)), ((1,), (1,))), preferred_e...  7.25 us
    dot_general x1, matrix products, per_device(): lax.dot_general(weighted, codes.astype(jnp.float32), (((2,), (0,)), ((0,)...  6.3 us
  transfers between devices with their start and end apart: 2, of which 2 were waited for; matrix products, arithmetic and copies ran while one was open for 0% of the time, Pallas kernels for 0%

commit v1 on v0

--- a/solution.py
+++ b/solution.py
@@ -24,7 +24,7 @@
         weighted, codes.astype(jnp.float32), (((2,), (0,)), ((0,), (1,))), precision=HIGH
     )
     local_proj = term.transpose(1, 0, 2).reshape(orthonormal.shape[0], block_count * 128)
-    projected = lax.psum(local_proj, "path")
+    projected = jnp.sum(lax.all_gather(local_proj, "path"), axis=0)
     total_paths = row_count * lax.axis_size("path")
     basis = orthonormal * jnp.sqrt(jnp.float32(total_paths))
     return (basis, projected)

time: 294 us -> 228 us (0.78)
  waiting for transfers between devices: 207 us -> 139 us
    psum x1 -> x0, waiting for transfers between devices: 109 us -> none  [per_device(): projected = lax.psum(local_proj, 'path')]
    all_gather x0 -> x1, waiting for transfers between devices: none -> 41.3 us  [per_device(): projected = jnp.sum(lax.all_gather(local_proj, 'path'), axis=0)]
where the time goes in v1:
time: 228 us; the launch traced here: 227 us
  waiting for transfers between devices  139 us (61%)
  blocking collectives  45.4 us (20%)
  matrix products  17.8 us (8%)
  between operations  14.1 us (6%)
  other arithmetic  9.06 us (4%)
    psum x1, waiting for transfers between devices, per_device(): sketched = lax.psum(partial_value, 'col')  97.9 us
    psum x1, blocking collectives, per_device(): gram_total = lax.psum(jnp.dot(sketched, sketched.T, precision=HIGH), 'path')  45.4 us
    all_gather x1, waiting for transfers between devices, per_device(): projected = jnp.sum(lax.all_gather(local_proj, 'path'), axis=0)  41.3 us
    dot_general x1, matrix products, per_device(): lax.dot_general(sketch3, codes, (((2,), (2,)), ((1,), (1,))), preferred_e...  7.25 us
    dot_general x1, matrix products, per_device(): lax.dot_general(weighted, codes.astype(jnp.float32), (((2,), (0,)), ((0,)...  6.3 us
  transfers between devices with their start and end apart: 2, of which 2 were waited for; matrix products, arithmetic and copies ran while one was open for 0% of the time, Pallas kernels for 0%

profile of v1, /device:TPU:1, one launch (start us, length us, event | category | flops | bytes accessed | tf_op | source)
XLA Modules:
  0.0 227.3 jit_solution(17306317051651105078)
XLA Ops:
  7.2 0.0 copy-start
  7.2 0.0 copy-start.1
  7.2 0.0 all-reduce.2.cloned.1.call-start
  7.2 0.8 copy-done
  8.0 7.3 %fusion.12 = f32[32,4096]{1,0:T(8,128)} fusion(f32[8,4096]{1,0:T(8,128)} %param.4, bf16[4096,1024]{1,0:T(8,128)(2,1)} %param.3, bf16[32,1024]{1,0:T(8,128)(2,1)S(1)} %copy-done), kind=kOutput, calls=%fused_computation.10 | convolution fusion | flops 270401536 | bytes 9109504 | tf_op jit(solution)/shard_map/dot_general | solution.py:14
  15.3 0.0 all-reduce.2.cloned.1.call-update
  15.3 0.0 all-gather.2.cloned.1.call-start
  15.3 97.9 %all-reduce.2.cloned.1.call-done = f32[32,4096]{1,0:T(8,128)} async-done(((f32[32,4096]{1,0:T(8,128)}), f32[32,4096]{1,0:T(8,128)}) %all-reduce.2.cloned.1.call-update) | async-done | bytes 524304 | tf_op jit(solution)/shard_map/psum | solution.py:18
  113.2 1.8 fusion.26
  115.0 45.4 %psum.15 = f32[32,32]{0,1:T(8,128)S(1)} all-reduce(f32[32,32]{0,1:T(8,128)S(1)} %fusion.26), channel_id=1, replica_groups=mesh['path'=16,'col'=16] {'path'}, use_global_device_ids=true, to_apply=%region_2.0 | all-reduce | flops 1024 | bytes 8192 | tf_op jit(solution)/shard_map/psum | solution.py:19
  160.4 0.1 copy.19
  160.5 2.9 %cholesky.16 = f32[32,32]{1,0:T(8,128)S(1)} custom-call(f32[32,32]{1,0:T(8,128)S(1)} %fusion.25), custom_call_target="Cholesky" | custom-call | tf_op jit(solution)/shard_map/jit(cholesky)/cholesky | solution.py:20
  163.5 0.6 compare_reduce_fusion
  164.1 0.7 fusion.22
  164.8 2.4 %custom-call.6 = f32[1,32,32]{1,2,0:T(8,128)S(1)} custom-call(f32[1,32,32]{2,1,0:T(8,128)S(1)} %fusion.22), custom_call_target="InvertDiagBlocksLowerTriangular" | custom-call | tf_op jit(solution)/shard_map/triangular_solve | solution.py:21
  167.2 2.5 %broadcast_multiply_fusion = (f32[32,4096]{1,0:T(8,128)}, f32[32,4096]{1,0:T(8,128)S(1)}) fusion(f32[32,4096]{1,0:T(8,128)} %all-reduce.2.cloned.1.call-done, f32[1,32,32]{1,2,0:T(8,128)S(1)} %custom-call.6), kind=kOutput, calls=%fused_computation.12 | convolution fusion | flops 50462720 | bytes 1576960 | tf_op jit(solution)/shard_map/triangular_solve | solution.py:21
  169.7 0.0 copy-done.1
  169.7 6.3 %fusion.15 = f32[32,8,128]{2,0,1:T(8,128)S(1)} fusion(f32[32,4096]{1,0:T(8,128)S(1)} %get-tuple-element.3, f32[8,4096]{1,0:T(8,128)S(1)} %copy-done.1, bf16[4096,1024]{1,0:T(8,128)(2,1)} %param.3), kind=kOutput, calls=%fused_computation.11 | convolution fusion | flops 1611661312 | bytes 9175040 | tf_op jit(solution)/shard_map/dot_general | solution.py:23
  176.0 0.1 copy.21
  176.1 0.7 all_gather_reshape.3
  176.8 0.0 all-gather.2.cloned.1.call-update
  176.8 41.3 %all-gather.2.cloned.1.call-done = f32[16,32,1024]{2,1,0:T(8,128)} async-done(((f32[1,32,1024]{2,1,0:T(8,128)}), f32[16,32,1024]{2,1,0:T(8,128)}) %all-gather.2.cloned.1.call-update) | async-done | bytes 2097168 | tf_op jit(solution)/shard_map/all_gather | solution.py:27
  218.1 2.4 %reduce_sum.19 = f32[32,1024]{1,0:T(8,128)} reduce(f32[16,32,1024]{2,1,0:T(8,128)} %all-gather.2.cloned.1.call-done, f32[]{:T(128)} %constant.39.clone.1), dimensions={0}, to_apply=%region_5.6 | reduce | flops 491520 | bytes 2228228 | tf_op jit(solution)/shard_map/reduce_sum | solution.py:27
  (2 shorter events, 0.0 us)
Async XLA Ops:
  7.2 0.8 copy-start
  7.2 162.5 %copy-start.1 = (f32[8,4096]{1,0:T(8,128)S(1)}, f32[8,4096]{1,0:T(8,128)}, u32[]{:S(2)}) copy-start(f32[8,4096]{1,0:T(8,128)} %param.4) | copy-start | bytes 393220
  7.2 106.0 %all-reduce.2.cloned.1.call-start = ((), (), s32[]{:S(2)}) async-start(), calls=%async_computation | async-start | bytes 1048576 | tf_op jit(solution)/shard_map/psum | solution.py:18
  15.3 202.8 %all-gather.2.cloned.1.call-start = ((), (), s32[]{:S(2)}) async-start(), calls=%async_computation.1 | async-start | bytes 2228224 | tf_op jit(solution)/shard_map/all_gather | solution.py:27
Sparse Core Ops, SparseCore 0:
  15.4 97.7 all-reduce.1
  176.9 41.1 all-gather.1
